TPU v7x, 512 devices: a whole 4x4x16 slice. The times are simulated.
512 devices in a mesh: vocab: 16 (over z), rows: 32 (over y, x, core).
Axes of the slice: x: 4, y: 4, z: 16, core: 2. Of those that a mesh axis runs over, the one named last changes fastest.
Arguments:
- trunk_hidden: bfloat16 [128, 7168], P('rows'), may hold values from -8 to 8
- mtp_state: bfloat16 [128, 7168], P('rows'), may hold values from -24 to 24, as said below
- mtp_gain: bfloat16 [7168], replicated, may hold values from 0.099609375 to 1.8984375
- head_weight: bfloat16 [73728, 7168], P(('vocab', 'rows')), may hold values from -0.28347335 to 0.28347335, as said below
- target_ids: int32 [128], replicated, may hold values from 0 to 73727
- mtp_target_ids: int32 [128], replicated, may hold values from 0 to 73727
- attn_values: bfloat16 [128, 64, 128], P('rows'), may hold values from -6 to 6
- out_proj: bfloat16 [8192, 7168], P('rows', 'vocab'), may hold values from -0.0625 to 0.0625
Outputs:
- grad_trunk: bfloat16 [128, 7168], P('rows')
- grad_residual: bfloat16 [128, 7168], P('rows')
- grad_gain: float32 [7168], replicated
- grad_head: bfloat16 [73728, 7168], P(('vocab', 'rows'))
- grad_attn: bfloat16 [128, 64, 128], P('vocab', 'rows')
- grad_out_proj: bfloat16 [8192, 7168], P('rows', 'vocab')
Inputs may be any that keep to these rules, and one draw needn't show every extreme that they name: `mtp_state`: block outputs; rows differ in scale. `head_weight`: head rows.
All inputs are finite; a program needn't handle non-finite values.
Results may differ from a plain program's by a relative error of at most 0.025.
Values may be sent and summed in bfloat16 or wider, within the bound.
A program may use at most 64 MiB of HBM per device.

v0:
```python
import jax
import jax.numpy as jnp
from jax import lax
from jax.sharding import PartitionSpec as P

loss_scale = 8.0
mtp_share = 0.3
norm_eps = 1e-06


def normalize(state):
    values = state.astype(jnp.float32)
    inverse = lax.rsqrt(jnp.mean(values * values, axis=-1, keepdims=True) + norm_eps)
    return (values * inverse, inverse)


def local(
    trunk_hidden,
    mtp_state,
    mtp_gain,
    head_weight,
    target_ids,
    mtp_target_ids,
    attn_values,
    out_proj,
):
    tok_local = trunk_hidden.shape[0]
    row_count = lax.axis_size("rows")
    vocab_rows = head_weight.shape[0]
    gain = mtp_gain.astype(jnp.float32)
    normed, inverse = normalize(mtp_state)
    mtp_hidden = (normed * gain).astype(jnp.bfloat16)
    stacked = jnp.concatenate([trunk_hidden, mtp_hidden], axis=0)
    targets = jnp.stack(
        [target_ids.reshape(row_count, tok_local), mtp_target_ids.reshape(row_count, tok_local)],
        axis=1,
    ).reshape(-1)
    shares = jnp.stack(
        [
            jnp.full((row_count, tok_local), loss_scale, jnp.float32),
            jnp.full((row_count, tok_local), loss_scale * mtp_share, jnp.float32),
        ],
        axis=1,
    ).reshape(-1)
    block_index = lax.axis_index("vocab") * row_count + lax.axis_index("rows")
    vocab_ids = block_index * vocab_rows + jnp.arange(vocab_rows, dtype=jnp.int32)
    onehot = (targets[:, None] == vocab_ids[None, :]).astype(jnp.float32)
    gathered = lax.all_gather(stacked, "rows", axis=0, tiled=True)
    logits = lax.dot_general(
        gathered, head_weight, (((1,), (1,)), ((), ())), preferred_element_type=jnp.float32
    )
    local_max = jnp.max(logits, axis=1)
    top = lax.pmax(local_max, ("vocab", "rows"))
    total = lax.psum(jnp.sum(jnp.exp(logits - top[:, None]), axis=1), ("vocab", "rows"))
    logit_grads = (
        shares[:, None] * (jnp.exp(logits - top[:, None]) / total[:, None] - onehot)
    ).astype(jnp.bfloat16)
    feature_width = out_proj.shape[1]
    column_start = lax.axis_index("vocab") * feature_width
    own_terms = lax.psum_scatter(
        jnp.dot(logit_grads, head_weight, preferred_element_type=jnp.float32).astype(jnp.bfloat16),
        "rows",
        scatter_dimension=0,
        tiled=True,
    )
    grad_hidden = lax.psum(own_terms, "vocab").astype(jnp.float32)
    head_total = lax.dot_general(
        logit_grads, gathered, (((0,), (0,)), ((), ())), preferred_element_type=jnp.float32
    )
    grad_head = head_total.astype(jnp.bfloat16)
    grad_trunk = grad_hidden[:tok_local].astype(jnp.bfloat16)
    mtp_grad = grad_hidden[tok_local:]
    grad_gain = lax.psum(jnp.sum(mtp_grad * normed, axis=0), "rows")
    scaled = mtp_grad * gain
    dot_mean = jnp.mean(scaled * normed, axis=-1, keepdims=True)
    grad_residual = (inverse * (scaled - normed * dot_mean)).astype(jnp.bfloat16)
    own_columns = lax.dynamic_slice_in_dim(grad_residual, column_start, feature_width, 1)
    all_columns = lax.all_gather(own_columns, "rows", axis=0, tiled=True)
    partial_attn = lax.dot_general(
        all_columns, out_proj, (((1,), (1,)), ((), ())), preferred_element_type=jnp.float32
    )
    attn_share = lax.psum_scatter(
        partial_attn.astype(jnp.bfloat16), "vocab", scatter_dimension=0, tiled=True
    ).astype(jnp.float32)
    head_count = out_proj.shape[0] // attn_values.shape[2]
    grad_attn = attn_share.astype(jnp.bfloat16).reshape(
        attn_share.shape[0], head_count, attn_values.shape[2]
    )
    proj_grads = jnp.einsum(
        "tkh,td->khd",
        lax.all_to_all(attn_values, "rows", split_axis=1, concat_axis=0, tiled=True),
        all_columns,
        preferred_element_type=jnp.float32,
    ).astype(jnp.bfloat16)
    grad_out_proj = proj_grads.reshape(out_proj.shape[0], feature_width)
    return (grad_trunk, grad_residual, grad_gain, grad_head, grad_attn, grad_out_proj)


def solution(mesh):
    return jax.shard_map(
        local,
        mesh=mesh,
        in_specs=(
            P("rows", None),
            P("rows", None),
            P(),
            P(("vocab", "rows"), None),
            P(),
            P(),
            P("rows", None, None),
            P("rows", "vocab"),
        ),
        out_specs=(
            P("rows", None),
            P("rows", None),
            P(),
            P(("vocab", "rows"), None),
            P("vocab", "rows", None),
            P("rows", "vocab"),
        ),
        check_vma=False,
    )
```

profile of v0, /device:TPU:32, one launch (start us, length us, event | category | flops | bytes accessed | tf_op | source)
XLA Modules:
  0.0 686.7 jit_solution(3278536386553361159)
XLA Ops:
  7.2 0.0 copy-start
  7.2 0.0 copy-start.5
  7.2 0.0 all-gather.3.cloned.1.call-start
  7.2 1.1 fusion.11
  8.4 0.7 convert_element_type.38
  9.1 0.9 fusion.9
  10.0 1.5 pad_maximum_fusion
  11.5 0.0 all-gather.3.cloned.1.call-update
  11.6 0.0 reduce-scatter.3.cloned.1.call-start
  11.6 0.8 stack_reshape.6
  12.4 0.8 stack_reshape.7
  13.2 0.1 eq.15
  13.3 63.5 %all-gather.3.cloned.1.call-done = bf16[256,7168]{1,0:T(8,128)(2,1)} async-done(((bf16[8,7168]{1,0:T(8,128)(2,1)}), bf16[256,7168]{1,0:T(8,128)(2,1)}) %all-gather.3.cloned.1.call-update) | async-done | bytes 3670032 | tf_op jit(solution)/shard_map/all_gather | solution.py:48
  76.8 0.0 copy-done
  76.8 3.4 fusion.13
  80.2 102.8 %pmax.7 = f32[256]{0:T(256)S(1)} all-reduce(f32[256]{0:T(256)S(1)} %get-tuple-element.32), channel_id=1, replica_groups=mesh['vocab'=16,'rows'=32] {'vocab','rows'}, use_global_device_ids=true, to_apply=%region_2.0 | all-reduce | flops 256 | bytes 2048 | tf_op jit(solution)/shard_map/pmax | solution.py:53
  183.0 101.3 %psum.21 = f32[256]{0:T(256)S(1)} all-reduce(f32[256]{0:T(256)S(1)} %fusion.5), channel_id=1, replica_groups=mesh['vocab'=16,'rows'=32] {'vocab','rows'}, use_global_device_ids=true, to_apply=%region_4.0 | all-reduce | flops 256 | bytes 2048 | tf_op jit(solution)/shard_map/psum | solution.py:54
  284.3 0.0 copy-done.5
  284.3 3.1 convolution_convert_fusion
  287.4 0.0 reduce-scatter.3.cloned.1.call-update
  287.4 0.0 copy-done.4
  287.4 0.0 copy-start.1
  287.4 0.0 copy-start.2
  287.5 0.7 copy.30
  288.1 4.3 all-to-all-start
  292.4 0.0 all-reduce.2.cloned.1.call-start
  292.5 7.4 %all-to-all-done = bf16[4,64,128]{2,0,1:T(4,128)(2,1)S(1)} async-done(((bf16[4,64,128]{2,0,1:T(4,128)(2,1)}), bf16[4,64,128]{2,0,1:T(4,128)(2,1)S(1)}, u32[]{:S(2)}, u32[]{:S(2)}) %all-to-all-start) | async-done | bytes 65568 | tf_op jit(solution)/shard_map/all_to_all | solution.py:91
  300.0 86.5 %reduce-scatter.3.cloned.1.call-done = bf16[8,7168]{1,0:T(8,128)(2,1)} async-done(((bf16[256,7168]{1,0:T(8,128)(2,1)}), bf16[8,7168]{1,0:T(8,128)(2,1)}) %reduce-scatter.3.cloned.1.call-update) | async-done | bytes 114704 | tf_op jit(solution)/shard_map/reduce_scatter | solution.py:60
  386.4 0.0 all-reduce.2.cloned.1.call-update
  386.4 0.0 reduce-scatter.5.cloned.1.call-start
  386.5 4.1 convolution_convert_fusion.1
  390.6 131.7 %all-reduce.2.cloned.1.call-done = bf16[8,7168]{1,0:T(8,128)(2,1)} async-done(((bf16[8,7168]{1,0:T(8,128)(2,1)}), bf16[8,7168]{1,0:T(8,128)(2,1)}) %all-reduce.2.cloned.1.call-update) | async-done | bytes 114704 | tf_op jit(solution)/shard_map/psum | solution.py:66
  522.3 0.0 copy-done.1
  522.3 1.2 fusion.12
  523.5 1.0 fusion.8
  524.5 0.0 copy-start.3
  524.5 0.1 dynamic-slice_bitcast_fusion
  524.6 24.6 %all-gather = bf16[32,4,448]{2,1,0:T(4,128)(2,1)S(1)} all-gather(bf16[1,4,448]{2,1,0:T(4,128)(2,1)S(1)} %dynamic-slice_bitcast_fusion), channel_id=1, replica_groups=mesh['vocab'=16,'rows'=32] {'rows'}, dimensions={0}, use_global_device_ids=true | all-gather | bytes 118272 | tf_op jit(solution)/shard_map/all_gather | solution.py:78
  549.2 0.1 reshape.41
  549.2 0.0 copy-done.2
  549.2 0.8 convolution_convert_fusion.3
  550.1 0.0 reduce-scatter.5.cloned.1.call-update
  550.1 0.2 fusion
  550.3 0.7 copy.39
  551.1 1.5 slice.13
  552.6 126.3 %psum.23 = f32[7168]{0:T(1024)} all-reduce(f32[7168]{0:T(1024)S(1)} %get-tuple-element.30), channel_id=1, replica_groups=mesh['vocab'=16,'rows'=32] {'rows'}, use_global_device_ids=true, to_apply=%region_9.0 | all-reduce | flops 7168 | bytes 57344 | tf_op jit(solution)/shard_map/psum | solution.py:73
  678.9 1.3 copy.34
  680.2 0.0 copy-done.3
  (9 shorter events, 0.1 us)
Async XLA Ops:
  7.2 69.6 %copy-start = (bf16[144,7168]{1,0:T(8,128)(2,1)S(1)}, bf16[144,7168]{1,0:T(8,128)(2,1)}, u32[]{:S(2)}) copy-start(bf16[144,7168]{1,0:T(8,128)(2,1)} %param.11) | copy-start | bytes 6193156
  7.2 277.2 %copy-start.5 = (f32[256]{0:T(256)S(1)}, f32[256]{0:T(256)}, u32[]{:S(2)}) copy-start(f32[256]{0:T(256)} %constant.6.clone.1) | copy-start | bytes 3076
  7.2 69.6 %all-gather.3.cloned.1.call-start = ((), (), s32[]{:S(2)}) async-start(), calls=%async_computation.3 | async-start | bytes 3784704 | tf_op jit(solution)/shard_map/all_gather | solution.py:48
  11.6 374.8 %reduce-scatter.3.cloned.1.call-start = ((), (), s32[]{:S(2)}) async-start(), calls=%async_computation.4 | async-start | bytes 3784704 | tf_op jit(solution)/shard_map/reduce_scatter | solution.py:60
  284.3 3.1 copy-start.4
  287.4 234.9 %copy-start.1 = (bf16[4,7168]{1,0:T(4,128)(2,1)S(1)}, bf16[4,7168]{1,0:T(4,128)(2,1)}, u32[]{:S(2)}) copy-start(bf16[4,7168]{1,0:T(4,128)(2,1)} %param.9) | copy-start | bytes 172036
  287.4 261.8 %copy-start.2 = (bf16[256,448]{0,1:T(8,128)(2,1)S(1)}, bf16[256,448]{0,1:T(8,128)(2,1)}, u32[]{:S(2)}) copy-start(bf16[256,448]{0,1:T(8,128)(2,1)} %param.15) | copy-start | bytes 688132
  288.1 11.8 %all-to-all-start = ((bf16[4,64,128]{2,0,1:T(4,128)(2,1)}), bf16[4,64,128]{2,0,1:T(4,128)(2,1)S(1)}, u32[]{:S(2)}, u32[]{:S(2)}) async-start(bf16[4,64,128]{2,0,1:T(4,128)(2,1)} %copy.30), calls=%async_computation.2 | async-start | bytes 131072 | tf_op jit(solution)/shard_map/all_to_all | solution.py:91
  292.4 229.8 %all-reduce.2.cloned.1.call-start = ((), (), s32[]{:S(2)}) async-start(), calls=%async_computation.5 | async-start | bytes 229376 | tf_op jit(solution)/shard_map/psum | solution.py:66
  386.4 292.5 %reduce-scatter.5.cloned.1.call-start = ((), (), s32[]{:S(2)}) async-start(), calls=%async_computation.6 | async-start | bytes 69632 | tf_op jit(solution)/shard_map/reduce_scatter | solution.py:82
  524.5 155.7 %copy-start.3 = (bf16[4,7168]{1,0:T(4,128)(2,1)}, bf16[4,7168]{1,0:T(4,128)(2,1)S(1)}, u32[]{:S(2)}) copy-start(bf16[4,7168]{1,0:T(4,128)(2,1)S(1)} %fusion.8) | copy-start | bytes 172036
Sparse Core Ops, SparseCore 0:
  11.7 65.0 all-gather.2
  287.5 98.8 reduce-scatter.2
  388.9 133.3 all-reduce.1
  550.2 62.4 reduce-scatter.4
where the time goes:
time: 687 us
  blocking collectives  355 us (52%)
  waiting for transfers between devices  289 us (42%)
  between operations  13.9 us (2%)
  matrix products  11.6 us (2%)
    psum x1, waiting for transfers between devices, local(): grad_hidden = lax.psum(own_terms, 'vocab').astype(jnp.float32)  132 us
    psum x1, blocking collectives, local(): grad_gain = lax.psum(jnp.sum(mtp_grad * normed, axis=0), 'rows')  126 us
    pmax x1, blocking collectives, local(): top = lax.pmax(local_max, ('vocab', 'rows'))  103 us
    psum x1, blocking collectives, local(): lax.psum(jnp.sum(jnp.exp(logits - top[:, None]), axis=1), ('vocab', 'rows'))  101 us
    reduce_scatter x1, waiting for transfers between devices, local(): lax.psum_scatter(jnp.dot(logit_grads, head_weight, preferred_element_type...  86.5 us
    all_gather x1, waiting for transfers between devices, local(): gathered = lax.all_gather(stacked, 'rows', axis=0, tiled=True)  63.5 us
    all_gather x1, blocking collectives, local(): all_columns = lax.all_gather(own_columns, 'rows', axis=0, tiled=True)  24.6 us
  transfers between devices with their start and end apart: 5, of which 4 were waited for; matrix products, arithmetic and copies ran while one was open for 1% of the time, Pallas kernels for 0%

commit v1 on v0

--- a/solution.py
+++ b/solution.py
@@ -51,7 +51,7 @@
     )
     local_max = jnp.max(logits, axis=1)
     top = lax.pmax(local_max, ("vocab", "rows"))
-    total = lax.psum(jnp.sum(jnp.exp(logits - top[:, None]), axis=1), ("vocab", "rows"))
+    total = lax.psum(lax.psum(jnp.sum(jnp.exp(logits - top[:, None]), axis=1), "rows"), "vocab")
     logit_grads = (
         shares[:, None] * (jnp.exp(logits - top[:, None]) / total[:, None] - onehot)
     ).astype(jnp.bfloat16)

time: 687 us -> 678 us (0.987)
  blocking collectives: 355 us -> 347 us
    psum x1 -> x2, blocking collectives: 101 us -> 92.9 us  [the longest x1 64 us: local(): lax.psum(jnp.sum(jnp.exp(logits - top[:, None]), axis=1), 'rows')]
where the time goes in v1:
time: 678 us; the launch traced here: 677 us
  blocking collectives  347 us (51%)
  waiting for transfers between devices  289 us (43%)
  between operations  13.9 us (2%)
  matrix products  11.6 us (2%)
    psum x1, waiting for transfers between devices, local(): grad_hidden = lax.psum(own_terms, 'vocab').astype(jnp.float32)  132 us
    psum x1, blocking collectives, local(): grad_gain = lax.psum(jnp.sum(mtp_grad * normed, axis=0), 'rows')  126 us
    pmax x1, blocking collectives, local(): top = lax.pmax(local_max, ('vocab', 'rows'))  103 us
    reduce_scatter x1, waiting for transfers between devices, local(): lax.psum_scatter(jnp.dot(logit_grads, head_weight, preferred_element_type...  86 us
    psum x1, blocking collectives, local(): lax.psum(jnp.sum(jnp.exp(logits - top[:, None]), axis=1), 'rows')  64 us
    all_gather x1, waiting for transfers between devices, local(): gathered = lax.all_gather(stacked, 'rows', axis=0, tiled=True)  63.5 us
    psum x1, blocking collectives, local(): lax.psum(lax.psum(jnp.sum(jnp.exp(logits - top[:, None]), axis=1), 'rows'...  28.9 us
    all_gather x1, blocking collectives, local(): all_columns = lax.all_gather(own_columns, 'rows', axis=0, tiled=True)  24.6 us
  transfers between devices with their start and end apart: 5, of which 4 were waited for; matrix products, arithmetic and copies ran while one was open for 1% of the time, Pallas kernels for 0%

profile of v1, /device:TPU:32, one launch (start us, length us, event | category | flops | bytes accessed | tf_op | source)
XLA Modules:
  0.0 677.4 jit_solution(5068430269895691938)
XLA Ops:
  7.2 0.0 copy-start
  7.2 0.0 copy-start.5
  7.2 0.0 all-gather.3.cloned.1.call-start
  7.2 1.1 fusion.11
  8.4 0.7 convert_element_type.38
  9.1 0.9 fusion.9
  10.0 1.5 pad_maximum_fusion
  11.5 0.0 all-gather.3.cloned.1.call-update
  11.6 0.0 reduce-scatter.3.cloned.1.call-start
  11.6 0.8 stack_reshape.6
  12.4 0.8 stack_reshape.7
  13.2 0.1 eq.15
  13.3 63.5 %all-gather.3.cloned.1.call-done = bf16[256,7168]{1,0:T(8,128)(2,1)} async-done(((bf16[8,7168]{1,0:T(8,128)(2,1)}), bf16[256,7168]{1,0:T(8,128)(2,1)}) %all-gather.3.cloned.1.call-update) | async-done | bytes 3670032 | tf_op jit(solution)/shard_map/all_gather | solution.py:48
  76.8 0.0 copy-done
  76.8 3.4 fusion.13
  80.2 102.8 %pmax.7 = f32[256]{0:T(256)S(1)} all-reduce(f32[256]{0:T(256)S(1)} %get-tuple-element.32), channel_id=1, replica_groups=mesh['vocab'=16,'rows'=32] {'vocab','rows'}, use_global_device_ids=true, to_apply=%region_2.0 | all-reduce | flops 256 | bytes 2048 | tf_op jit(solution)/shard_map/pmax | solution.py:53
  183.0 64.0 %psum.28 = f32[256]{0:T(256)S(1)} all-reduce(f32[256]{0:T(256)S(1)} %fusion.5), channel_id=1, replica_groups=mesh['vocab'=16,'rows'=32] {'rows'}, use_global_device_ids=true, to_apply=%region_4.0 | all-reduce | flops 256 | bytes 2048 | tf_op jit(solution)/shard_map/psum | solution.py:54
  247.0 28.9 %psum.29 = f32[256]{0:T(256)S(1)} all-reduce(f32[256]{0:T(256)S(1)} %psum.28), channel_id=1, replica_groups=mesh['vocab'=16,'rows'=32] {'vocab'}, use_global_device_ids=true, to_apply=%region_5.0 | all-reduce | flops 256 | bytes 2048 | tf_op jit(solution)/shard_map/psum | solution.py:54
  275.9 0.0 copy-done.5
  275.9 3.1 convolution_convert_fusion
  278.9 0.0 reduce-scatter.3.cloned.1.call-update
  279.0 0.0 copy-done.4
  279.0 0.0 copy-start.1
  279.0 0.0 copy-start.2
  279.0 0.7 copy.30
  279.7 3.9 all-to-all-start
  283.5 0.0 all-reduce.2.cloned.1.call-start
  283.6 7.4 %all-to-all-done = bf16[4,64,128]{2,0,1:T(4,128)(2,1)S(1)} async-done(((bf16[4,64,128]{2,0,1:T(4,128)(2,1)}), bf16[4,64,128]{2,0,1:T(4,128)(2,1)S(1)}, u32[]{:S(2)}, u32[]{:S(2)}) %all-to-all-start) | async-done | bytes 65568 | tf_op jit(solution)/shard_map/all_to_all | solution.py:91
  291.0 86.0 %reduce-scatter.3.cloned.1.call-done = bf16[8,7168]{1,0:T(8,128)(2,1)} async-done(((bf16[256,7168]{1,0:T(8,128)(2,1)}), bf16[8,7168]{1,0:T(8,128)(2,1)}) %reduce-scatter.3.cloned.1.call-update) | async-done | bytes 114704 | tf_op jit(solution)/shard_map/reduce_scatter | solution.py:60
  377.1 0.0 all-reduce.2.cloned.1.call-update
  377.1 0.0 reduce-scatter.5.cloned.1.call-start
  377.1 4.1 convolution_convert_fusion.1
  381.2 131.7 %all-reduce.2.cloned.1.call-done = bf16[8,7168]{1,0:T(8,128)(2,1)} async-done(((bf16[8,7168]{1,0:T(8,128)(2,1)}), bf16[8,7168]{1,0:T(8,128)(2,1)}) %all-reduce.2.cloned.1.call-update) | async-done | bytes 114704 | tf_op jit(solution)/shard_map/psum | solution.py:66
  512.9 0.0 copy-done.1
  512.9 1.2 fusion.12
  514.2 1.0 fusion.8
  515.2 0.0 copy-start.3
  515.2 0.1 dynamic-slice_bitcast_fusion
  515.3 24.6 %all-gather = bf16[32,4,448]{2,1,0:T(4,128)(2,1)S(1)} all-gather(bf16[1,4,448]{2,1,0:T(4,128)(2,1)S(1)} %dynamic-slice_bitcast_fusion), channel_id=1, replica_groups=mesh['vocab'=16,'rows'=32] {'rows'}, dimensions={0}, use_global_device_ids=true | all-gather | bytes 118272 | tf_op jit(solution)/shard_map/all_gather | solution.py:78
  539.8 0.1 reshape.41
  539.9 0.0 copy-done.2
  539.9 0.8 convolution_convert_fusion.3
  540.7 0.0 reduce-scatter.5.cloned.1.call-update
  540.7 0.2 fusion
  541.0 0.7 copy.39
  541.7 1.5 slice.13
  543.3 126.3 %psum.31 = f32[7168]{0:T(1024)} all-reduce(f32[7168]{0:T(1024)S(1)} %get-tuple-element.30), channel_id=1, replica_groups=mesh['vocab'=16,'rows'=32] {'rows'}, use_global_device_ids=true, to_apply=%region_10.0 | all-reduce | flops 7168 | bytes 57344 | tf_op jit(solution)/shard_map/psum | solution.py:73
  669.6 1.3 copy.34
  (10 shorter events, 0.1 us)
Async XLA Ops:
  7.2 69.6 %copy-start = (bf16[144,7168]{1,0:T(8,128)(2,1)S(1)}, bf16[144,7168]{1,0:T(8,128)(2,1)}, u32[]{:S(2)}) copy-start(bf16[144,7168]{1,0:T(8,128)(2,1)} %param.11) | copy-start | bytes 6193156
  7.2 268.7 %copy-start.5 = (f32[256]{0:T(256)S(1)}, f32[256]{0:T(256)}, u32[]{:S(2)}) copy-start(f32[256]{0:T(256)} %constant.6.clone.1) | copy-start | bytes 3076
  7.2 69.6 %all-gather.3.cloned.1.call-start = ((), (), s32[]{:S(2)}) async-start(), calls=%async_computation.3 | async-start | bytes 3784704 | tf_op jit(solution)/shard_map/all_gather | solution.py:48
  11.6 365.5 %reduce-scatter.3.cloned.1.call-start = ((), (), s32[]{:S(2)}) async-start(), calls=%async_computation.4 | async-start | bytes 3784704 | tf_op jit(solution)/shard_map/reduce_scatter | solution.py:60
  275.9 3.1 copy-start.4
  279.0 234.0 %copy-start.1 = (bf16[4,7168]{1,0:T(4,128)(2,1)S(1)}, bf16[4,7168]{1,0:T(4,128)(2,1)}, u32[]{:S(2)}) copy-start(bf16[4,7168]{1,0:T(4,128)(2,1)} %param.9) | copy-start | bytes 172036
  279.0 260.9 %copy-start.2 = (bf16[256,448]{0,1:T(8,128)(2,1)S(1)}, bf16[256,448]{0,1:T(8,128)(2,1)}, u32[]{:S(2)}) copy-start(bf16[256,448]{0,1:T(8,128)(2,1)} %param.15) | copy-start | bytes 688132
  279.7 11.3 %all-to-all-start = ((bf16[4,64,128]{2,0,1:T(4,128)(2,1)}), bf16[4,64,128]{2,0,1:T(4,128)(2,1)S(1)}, u32[]{:S(2)}, u32[]{:S(2)}) async-start(bf16[4,64,128]{2,0,1:T(4,128)(2,1)} %copy.30), calls=%async_computation.2 | async-start | bytes 131072 | tf_op jit(solution)/shard_map/all_to_all | solution.py:91
  283.5 229.4 %all-reduce.2.cloned.1.call-start = ((), (), s32[]{:S(2)}) async-start(), calls=%async_computation.5 | async-start | bytes 229376 | tf_op jit(solution)/shard_map/psum | solution.py:66
  377.1 292.5 %reduce-scatter.5.cloned.1.call-start = ((), (), s32[]{:S(2)}) async-start(), calls=%async_computation.6 | async-start | bytes 69632 | tf_op jit(solution)/shard_map/reduce_scatter | solution.py:82
  515.2 155.7 %copy-start.3 = (bf16[4,7168]{1,0:T(4,128)(2,1)}, bf16[4,7168]{1,0:T(4,128)(2,1)S(1)}, u32[]{:S(2)}) copy-start(bf16[4,7168]{1,0:T(4,128)(2,1)S(1)} %fusion.8) | copy-start | bytes 172036
Sparse Core Ops, SparseCore 0:
  11.7 65.0 all-gather.2
  279.1 97.9 reduce-scatter.2
  379.5 133.3 all-reduce.1
  540.9 62.4 reduce-scatter.4
